TPU v7x, 32 devices: a whole 2x2x4 slice. The times are simulated.
32 devices in a mesh: rotor: 4 (over y, core), blk: 8 (over z, x).
Axes of the slice: x: 2, y: 2, z: 4, core: 2. Of those that a mesh axis runs over, the one named last changes fastest.
Arguments:
- positions: float32 [3, 131072], P(None, ('rotor', 'blk')), may hold values from -6 to 6
- strengths: float32 [3, 131072], P(None, ('rotor', 'blk'))
- blade_of_block: int32 [1024], P(('rotor', 'blk')), may hold values from 0 to 29
- circulation: float32 [30], replicated, may hold values from 0.5 to 2
- tile_source_dev: int32 [8192, 1], P(('rotor', 'blk')), may hold values from 0 to 31; in each aligned block of 256 rows (0 to 255, 256 to 511, ...) at most 12 rows name the same one
- tile_source_blk: int32 [8192], P(('rotor', 'blk')), may hold values from 0 to 31
- tile_target: int32 [8192], P(('rotor', 'blk')), may hold values from 0 to 31
- tile_count: int32 [32], P(('rotor', 'blk')), may hold values from 128 to 256, as said below
Outputs:
- velocity: float32 [3, 131072], P(None, ('rotor', 'blk'))
- strength_rate: float32 [3, 131072], P(None, ('rotor', 'blk'))
Inputs may be any that keep to these rules, and one draw needn't show every extreme that they name: `tile_source_dev`: among the 256 slots of one device no device number appears more than 12 times, and one appears exactly 12 times. `tile_count`: some device has all 256 slots live.
All inputs are finite; a program needn't handle non-finite values.
Results may differ from a plain program's by a relative error of at most 0.0003.
Values sent between devices are 32-bit elements; how exact they have to be, the bound alone decides.
A program may use at most 128 MiB of HBM per device.

v0:
```python
import math
import jax
import jax.numpy as jnp
from jax import lax
from jax.sharding import PartitionSpec as P

inverse_four_pi = 1.0 / (4.0 * math.pi)
core_square = 1.0
diffusion_rate = 2.0
highest = lax.Precision.HIGHEST


def with_halo(cells, sides, width):
    for axis, dim in sides:
        count = lax.axis_size(axis)
        ends = count - 1
        head = lax.slice_in_dim(cells, 0, width, axis=dim)
        tail = lax.slice_in_dim(cells, cells.shape[dim] - width, cells.shape[dim], axis=dim)
        cells = jnp.concatenate(
            [
                lax.ppermute(tail, axis, [(i, (i + 1) % count) for i in range(ends)]),
                cells,
                lax.ppermute(head, axis, [((i + 1) % count, i) for i in range(ends)]),
            ],
            axis=dim,
        )
    return cells


def cross_rows(left, right):
    return jnp.stack(
        [
            left[1] * right[2] - left[2] * right[1],
            left[2] * right[0] - left[0] * right[2],
            left[0] * right[1] - left[1] * right[0],
        ]
    )


def contract(matrix, values):
    return jnp.einsum("ts,cs->ct", matrix, values, precision=highest)


def kernels(target_pos, source_pos):
    offset_vec = target_pos[:, :, None] - source_pos[:, None, :]
    distance_sq = jnp.sum(offset_vec * offset_vec, axis=0)
    inverse = 1.0 / (distance_sq + core_square)
    green_kernel = inverse_four_pi * inverse * jnp.sqrt(inverse)
    return (green_kernel, 3.0 * green_kernel * inverse, jnp.exp(-distance_sq / core_square))


def toward(target, source, green_kernel, hessian, smooth):
    target_pos, target_str = (target[:3], target[3:])
    source_pos, source_str = (source[:3], source[3:])
    spin_src = cross_rows(source_pos, source_str)
    green_str = contract(green_kernel, source_str)
    velocity = contract(green_kernel, spin_src) - cross_rows(target_pos, green_str)
    along_axis = jnp.sum(target_str * target_pos, axis=0)[:, None] - jnp.einsum(
        "ct,cs->ts", target_str, source_pos, precision=highest
    )
    lever_arm = hessian * along_axis
    stretch = (
        cross_rows(target_pos, contract(lever_arm, source_str))
        - contract(lever_arm, spin_src)
        - cross_rows(target_str, green_str)
    )
    diffusion = contract(smooth, source_str) - jnp.sum(smooth, axis=1)[None, :] * target_str
    return jnp.concatenate([velocity, stretch + diffusion_rate * diffusion], axis=0)


def near_block(target, sources, validity):
    green_kernel, hessian, smooth = kernels(target[:3], sources[:3])
    return toward(target, sources, green_kernel, hessian, smooth * validity[None, :])


def tile_pair(target, source):
    green_kernel, hessian, smooth = kernels(target[:3], source[:3])
    forward = toward(target, source, green_kernel, hessian, smooth)
    backward = toward(source, target, green_kernel.T, hessian.T, smooth.T)
    return (forward, backward)


def send_requests(request):
    return lax.all_to_all(request, ("rotor", "blk"), split_axis=0, concat_axis=0, tiled=True)


def send_blocks(outgoing):
    return lax.all_to_all(outgoing, ("rotor", "blk"), split_axis=0, concat_axis=0, tiled=True)


def send_results(results):
    return lax.all_to_all(results, ("rotor", "blk"), split_axis=0, concat_axis=0, tiled=True)


def local(
    positions,
    strengths,
    blade_of_block,
    circulation,
    tile_source_dev,
    tile_source_blk,
    tile_target,
    tile_count,
):
    local_blocks = blade_of_block.shape[0]
    width = positions.shape[1] // local_blocks
    n_rotor = lax.axis_size("rotor")
    n_blk = lax.axis_size("blk")
    devices = n_rotor * n_blk
    magnitude = (
        jnp.sqrt(jnp.sum(strengths * strengths, axis=0)).reshape(local_blocks, width).sum(axis=1)
    )
    member = (
        blade_of_block[:, None] == jnp.arange(circulation.shape[0], dtype=jnp.int32)[None, :]
    ).astype(jnp.float32)
    totals, counted = lax.psum(
        (jnp.sum(member * magnitude[:, None], axis=0), jnp.sum(member, axis=0) * width),
        ("rotor", "blk"),
    )
    factor = circulation / (totals / jnp.maximum(counted, 1.0) + 1e-06)
    block_factor = jnp.sum(member * factor[None, :], axis=1)
    scaled = strengths * jnp.repeat(block_factor, width)[None, :]
    state = jnp.concatenate([positions, scaled], axis=0)
    blocks = state.reshape(6, local_blocks, width).transpose(1, 0, 2)
    padded = with_halo(state, (("blk", 1),), width)
    place = lax.axis_index("blk")
    validity = jnp.concatenate(
        [
            jnp.full((width,), place > 0),
            jnp.ones((local_blocks * width,), bool),
            jnp.full((width,), place < n_blk - 1),
        ]
    ).astype(jnp.float32)

    def near_one(index):
        start = index * width
        sources = lax.dynamic_slice_in_dim(padded, start, 3 * width, 1)
        weights = lax.dynamic_slice_in_dim(validity, start, 3 * width, 0)
        return near_block(blocks[index], sources, weights)

    near_group = math.gcd(local_blocks, 16)
    near = lax.map(
        jax.vmap(near_one), jnp.arange(local_blocks, dtype=jnp.int32).reshape(-1, near_group)
    )
    near = near.reshape(local_blocks, 6, width)
    capacity = tile_target.shape[0]
    slot_count = max(2, (3 * capacity + 2 * devices - 1) // (2 * devices))
    source_dev = tile_source_dev[:, 0]
    positions_idx = jnp.arange(capacity, dtype=jnp.int32)
    live_tile = (positions_idx < tile_count[0]).astype(jnp.float32)
    same_peer = (source_dev[:, None] == source_dev[None, :]) & (
        positions_idx[:, None] > positions_idx[None, :]
    )
    rank_in_peer = jnp.sum(same_peer.astype(jnp.int32), axis=1)
    slot_index = source_dev * slot_count + rank_in_peer
    wanted = (
        slot_index[None, :] == jnp.arange(devices * slot_count, dtype=jnp.int32)[:, None]
    ).astype(jnp.int32)
    request = (jnp.sum(wanted * (tile_source_blk[None, :] + 1), axis=1) - 1).reshape(
        devices, slot_count
    )
    asked = send_requests(request)
    present = (asked >= 0).astype(jnp.float32)
    outgoing = blocks[jnp.clip(asked, 0, local_blocks - 1)] * present[:, :, None, None]
    incoming = send_blocks(outgoing)
    sources = incoming.reshape(devices * slot_count, 6, width)[slot_index]
    targets = blocks[tile_target]
    tile_batch = math.gcd(capacity, 64)
    groups = capacity // tile_batch

    def tile_group(pair):
        return jax.vmap(tile_pair)(pair[0], pair[1])

    target_out, source_out = lax.map(
        tile_group,
        (
            targets.reshape(groups, tile_batch, 6, width),
            sources.reshape(groups, tile_batch, 6, width),
        ),
    )
    target_out = target_out.reshape(capacity, 6, width) * live_tile[:, None, None]
    source_out = source_out.reshape(capacity, 6, width) * live_tile[:, None, None]
    target_hot = (
        tile_target[None, :] == jnp.arange(local_blocks, dtype=jnp.int32)[:, None]
    ).astype(jnp.float32)
    cross_target = jnp.einsum("nc,cxp->nxp", target_hot, target_out, precision=highest)
    back = jnp.einsum("fc,cxp->fxp", wanted.astype(jnp.float32), source_out, precision=highest)
    returned = send_results(back.reshape(devices, slot_count, 6, width))
    return_hot = (
        asked.reshape(-1)[None, :] == jnp.arange(local_blocks, dtype=jnp.int32)[:, None]
    ).astype(jnp.float32)
    cross_source = jnp.einsum(
        "nf,fxp->nxp",
        return_hot,
        returned.reshape(devices * slot_count, 6, width),
        precision=highest,
    )
    total = near + cross_target + cross_source
    flat_terms = total.transpose(1, 0, 2).reshape(6, local_blocks * width)
    return (flat_terms[:3], flat_terms[3:])


def solution(mesh):
    placed = (
        P(None, ("rotor", "blk")),
        P(None, ("rotor", "blk")),
        P(("rotor", "blk")),
        P(),
        P(("rotor", "blk"), None),
        P(("rotor", "blk")),
        P(("rotor", "blk")),
        P(("rotor", "blk")),
    )
    return jax.shard_map(
        local,
        mesh=mesh,
        in_specs=placed,
        out_specs=(P(None, ("rotor", "blk")), P(None, ("rotor", "blk"))),
        check_vma=False,
    )
```

profile of v0, /device:TPU:0, one launch (start us, length us, event | category | flops | bytes accessed | tf_op | source)
XLA Modules:
  0.0 721.0 jit_solution(6770685092090512786)
XLA Ops:
  3.7 7.3 %all-to-all-start = ((s32[32,1,12]{2,1,0:T(1,128)}), s32[32,1,12]{2,1,0:T(1,128)S(1)}, u32[]{:S(2)}, u32[]{:S(2)}) async-start(s32[32,1,12]{2,1,0:T(1,128)} %bitcast.65), calls=%async_computation | async-start | bytes 32768 | tf_op jit(solution)/shard_map/all_to_all | solution.py:84
  12.7 40.5 %all-reduce.2 = (f32[30]{0:T(128)S(1)}, f32[30]{0:T(128)S(1)}) all-reduce(f32[30]{0:T(128)S(1)} %get-tuple-element.104, f32[30]{0:T(128)S(1)} %broadcast_multiply_fusion.4), channel_id=1, replica_groups=mesh['rotor'=4,'blk'=8] {'rotor','blk'}, use_global_device_ids=true, to_apply=%region_3.0 | all-reduce | flops 60 | bytes 480 | tf_op jit(solution)/shard_map/psum | solution.py:116
  61.6 4.5 all-to-all-start.1
  66.7 4.3 collective-permute-start
  79.8 25.1 %all-to-all-done.1 = f32[32,12,6,128]{3,2,1,0:T(8,128)S(1)} async-done(((f32[32,12,6,128]{3,2,1,0:T(8,128)}), f32[32,12,6,128]{3,2,1,0:T(8,128)S(1)}, u32[]{:S(2)}, u32[]{:S(2)}) %all-to-all-start.1) | async-done | bytes 1179680 | tf_op jit(solution)/shard_map/all_to_all | solution.py:88
  107.1 416.8 %while.29 = (s32[]{:T(128)}, f32[4,64,6,128]{3,1,0,2:T(8,128)}, f32[4,64,6,128]{3,1,0,2:T(8,128)}, f32[4,64,6,128]{3,1,2,0:T(8,128)}, f32[4,64,6,128]{3,1,2,0:T(8,128)S(1)}, /*index=5*/s32[]{:T(128)}) while((s32[]{:T(128)}, f32[4,64,6,128]{3,1,0,2:T(8,128)}, f32[4,64,6,128]{3,1,0,2:T(8,128)}, f32[4,64,6,128]{3,1,2,0:T(8,128)}, ...), condition=%wide.region_20.21_spmd, body=%wide.region_14.20_spmd.sunk | while | flops 495419392 | bytes 144605344 | solution.py:174
  108.5 4.1 multiply_reduce_fusion.13
  116.2 6.6 fusion.211
  122.8 8.4 %fusion.214 = f32[64,128,128]{1,2,0:T(8,128)S(1)} fusion(f32[64,128]{1,0:T(8,128)S(1)} %get-tuple-element.490, f32[64,3,128]{2,0,1:T(8,128)S(1)} %get-tuple-element.473, f32[64,3,128]{2,0,1:T(8,128)S(1)} %get-tuple-element.469, f32[64,128,128]{2,1,0:T(8,128)S(1)} %multiply_reduce_fusion.13), kind=kOutput, calls=%fused_computation.10.clone.1 | convolution fusion | flops 46137344 | bytes 8617984 | tf_op jit(solution)/shard_map/while/body/eval_jaxpr/vmap(ct,cs->ts)/dot_general | solution.py:58
  142.0 5.6 copy.502
  147.6 9.2 %fusion.224 = f32[64,3,128]{2,1,0:T(4,128)S(1)} fusion(f32[64,128,128]{1,2,0:T(8,128)} %copy.502, f32[3,64,128]{2,1,0:T(8,128)S(1)} %pad_maximum_fusion.18), kind=kOutput, calls=%fused_computation.21.clone.1 | convolution fusion | flops 39845888 | bytes 4390912 | tf_op jit(solution)/shard_map/while/body/eval_jaxpr/vmap(ts,cs->ct)/dot_general | solution.py:41
  156.8 7.2 fusion.212
  164.0 4.5 fusion.209
  168.7 4.7 fusion.219
  176.8 5.6 copy.503
  182.4 10.4 %subtract_multiply_fusion.5 = f32[64,128,128]{2,1,0:T(8,128)S(1)} fusion(f32[64,128,128]{2,1,0:T(8,128)} %copy.503, f32[64,128]{1,0:T(8,128)S(1)} %get-tuple-element.471, f32[64,3,128]{2,0,1:T(8,128)S(1)} %get-tuple-element.472, f32[64,3,128]{2,0,1:T(8,128)S(1)} %get-tuple-element.468, f32[64,128,128]{2,1,0:T(8,128)} %copy-done.1), kind=kOutput, calls=%fused_computation.12.clone.1 | convolution fusion | flops 42991616 | bytes 12812288 | tf_op jit(solution)/shard_map/while/body/eval_jaxpr/vmap(ct,cs->ts)/dot_general | solution.py:58
  192.9 6.6 fusion.217
  199.4 6.6 fusion.207
  208.4 4.1 multiply_reduce_fusion.13
  216.1 6.6 fusion.211
  222.7 8.4 %fusion.214 = f32[64,128,128]{1,2,0:T(8,128)S(1)} fusion(f32[64,128]{1,0:T(8,128)S(1)} %get-tuple-element.490, f32[64,3,128]{2,0,1:T(8,128)S(1)} %get-tuple-element.473, f32[64,3,128]{2,0,1:T(8,128)S(1)} %get-tuple-element.469, f32[64,128,128]{2,1,0:T(8,128)S(1)} %multiply_reduce_fusion.13), kind=kOutput, calls=%fused_computation.10.clone.1 | convolution fusion | flops 46137344 | bytes 8617984 | tf_op jit(solution)/shard_map/while/body/eval_jaxpr/vmap(ct,cs->ts)/dot_general | solution.py:58
  241.9 5.6 copy.502
  247.5 9.2 %fusion.224 = f32[64,3,128]{2,1,0:T(4,128)S(1)} fusion(f32[64,128,128]{1,2,0:T(8,128)} %copy.502, f32[3,64,128]{2,1,0:T(8,128)S(1)} %pad_maximum_fusion.18), kind=kOutput, calls=%fused_computation.21.clone.1 | convolution fusion | flops 39845888 | bytes 4390912 | tf_op jit(solution)/shard_map/while/body/eval_jaxpr/vmap(ts,cs->ct)/dot_general | solution.py:41
  256.7 7.2 fusion.212
  263.9 4.5 fusion.209
  268.6 4.7 fusion.219
  276.7 5.6 copy.503
  282.3 10.4 %subtract_multiply_fusion.5 = f32[64,128,128]{2,1,0:T(8,128)S(1)} fusion(f32[64,128,128]{2,1,0:T(8,128)} %copy.503, f32[64,128]{1,0:T(8,128)S(1)} %get-tuple-element.471, f32[64,3,128]{2,0,1:T(8,128)S(1)} %get-tuple-element.472, f32[64,3,128]{2,0,1:T(8,128)S(1)} %get-tuple-element.468, f32[64,128,128]{2,1,0:T(8,128)} %copy-done.1), kind=kOutput, calls=%fused_computation.12.clone.1 | convolution fusion | flops 42991616 | bytes 12812288 | tf_op jit(solution)/shard_map/while/body/eval_jaxpr/vmap(ct,cs->ts)/dot_general | solution.py:58
  292.7 6.6 fusion.217
  299.3 6.6 fusion.207
  308.3 4.1 multiply_reduce_fusion.13
  315.9 6.6 fusion.211
  322.5 8.4 %fusion.214 = f32[64,128,128]{1,2,0:T(8,128)S(1)} fusion(f32[64,128]{1,0:T(8,128)S(1)} %get-tuple-element.490, f32[64,3,128]{2,0,1:T(8,128)S(1)} %get-tuple-element.473, f32[64,3,128]{2,0,1:T(8,128)S(1)} %get-tuple-element.469, f32[64,128,128]{2,1,0:T(8,128)S(1)} %multiply_reduce_fusion.13), kind=kOutput, calls=%fused_computation.10.clone.1 | convolution fusion | flops 46137344 | bytes 8617984 | tf_op jit(solution)/shard_map/while/body/eval_jaxpr/vmap(ct,cs->ts)/dot_general | solution.py:58
  341.7 5.6 copy.502
  347.3 9.2 %fusion.224 = f32[64,3,128]{2,1,0:T(4,128)S(1)} fusion(f32[64,128,128]{1,2,0:T(8,128)} %copy.502, f32[3,64,128]{2,1,0:T(8,128)S(1)} %pad_maximum_fusion.18), kind=kOutput, calls=%fused_computation.21.clone.1 | convolution fusion | flops 39845888 | bytes 4390912 | tf_op jit(solution)/shard_map/while/body/eval_jaxpr/vmap(ts,cs->ct)/dot_general | solution.py:41
  356.5 7.2 fusion.212
  363.8 4.5 fusion.209
  368.5 4.7 fusion.219
  376.5 5.6 copy.503
  382.2 10.4 %subtract_multiply_fusion.5 = f32[64,128,128]{2,1,0:T(8,128)S(1)} fusion(f32[64,128,128]{2,1,0:T(8,128)} %copy.503, f32[64,128]{1,0:T(8,128)S(1)} %get-tuple-element.471, f32[64,3,128]{2,0,1:T(8,128)S(1)} %get-tuple-element.472, f32[64,3,128]{2,0,1:T(8,128)S(1)} %get-tuple-element.468, f32[64,128,128]{2,1,0:T(8,128)} %copy-done.1), kind=kOutput, calls=%fused_computation.12.clone.1 | convolution fusion | flops 42991616 | bytes 12812288 | tf_op jit(solution)/shard_map/while/body/eval_jaxpr/vmap(ct,cs->ts)/dot_general | solution.py:58
  392.6 6.6 fusion.217
  399.2 6.6 fusion.207
  415.8 6.6 fusion.211
  422.4 8.4 %fusion.214 = f32[64,128,128]{1,2,0:T(8,128)S(1)} fusion(f32[64,128]{1,0:T(8,128)S(1)} %get-tuple-element.490, f32[64,3,128]{2,0,1:T(8,128)S(1)} %get-tuple-element.473, f32[64,3,128]{2,0,1:T(8,128)S(1)} %get-tuple-element.469, f32[64,128,128]{2,1,0:T(8,128)S(1)} %multiply_reduce_fusion.13), kind=kOutput, calls=%fused_computation.10.clone.1 | convolution fusion | flops 46137344 | bytes 8617984 | tf_op jit(solution)/shard_map/while/body/eval_jaxpr/vmap(ct,cs->ts)/dot_general | solution.py:58
  441.6 5.6 copy.502
  447.2 9.2 %fusion.224 = f32[64,3,128]{2,1,0:T(4,128)S(1)} fusion(f32[64,128,128]{1,2,0:T(8,128)} %copy.502, f32[3,64,128]{2,1,0:T(8,128)S(1)} %pad_maximum_fusion.18), kind=kOutput, calls=%fused_computation.21.clone.1 | convolution fusion | flops 39845888 | bytes 4390912 | tf_op jit(solution)/shard_map/while/body/eval_jaxpr/vmap(ts,cs->ct)/dot_general | solution.py:41
  456.4 7.2 fusion.212
  463.6 4.5 fusion.209
  468.3 4.7 fusion.219
  476.4 5.6 copy.503
  482.0 10.4 %subtract_multiply_fusion.5 = f32[64,128,128]{2,1,0:T(8,128)S(1)} fusion(f32[64,128,128]{2,1,0:T(8,128)} %copy.503, f32[64,128]{1,0:T(8,128)S(1)} %get-tuple-element.471, f32[64,3,128]{2,0,1:T(8,128)S(1)} %get-tuple-element.472, f32[64,3,128]{2,0,1:T(8,128)S(1)} %get-tuple-element.468, f32[64,128,128]{2,1,0:T(8,128)} %copy-done.1), kind=kOutput, calls=%fused_computation.12.clone.1 | convolution fusion | flops 42991616 | bytes 12812288 | tf_op jit(solution)/shard_map/while/body/eval_jaxpr/vmap(ct,cs->ts)/dot_general | solution.py:58
  492.5 6.6 fusion.217
  499.0 6.6 fusion.207
  531.9 186.4 %while.28 = (s32[]{:T(128)}, f32[2,16,6,128]{3,1,0,2:T(8,128)S(1)}, s32[2,16]{1,0:T(2,128)S(1)}, f32[6,4352]{1,0:T(8,128)}, f32[32,6,128]{2,1,0:T(8,128)S(1)}, /...) while((s32[]{:T(128)}, f32[2,16,6,128]{3,1,0,2:T(8,128)S(1)}, ...), condition=%wide.region_11.12_spmd, body=%wide.region_7.11_spmd.sunk | while | flops 192960656 | bytes 30571508 | solution.py:142
  531.9 32.7 %while.31 = (s32[]{:T(128)}, f32[4352]{0:T(1024)}, s32[16,1]{0,1:T(1,128)S(1)}, f32[16,384]{1,0:T(8,128)S(1)}, s32[]{:T(128)}, /*index=5*/s32[]{:T(128)}) while((s32[]{:T(128)}, f32[4352]{0:T(1024)}, s32[16,1]{0,1:T(1,128)S(1)}, f32[16,384]{1,0:T(8,128)S(1)}, s32[]{:T(128)}, /*index=5*/s32[]{:T(128)}) %tuple.176), condition=%wide.while_cond.1, body=%wide.while_body.1.sunk | while | flops 2 | bytes 9313 | solution.py:138
  565.3 32.7 %while.30 = (s32[]{:T(128)}, f32[6,4352]{1,0:T(8,128)}, s32[16,2]{0,1:T(2,128)S(1)}, f32[16,6,384]{2,1,0:T(8,128)S(1)}, s32[]{:T(128)}) while((s32[]{:T(128)}, f32[6,4352]{1,0:T(8,128)}, s32[16,2]{0,1:T(2,128)S(1)}, f32[16,6,384]{2,1,0:T(8,128)S(1)}, s32[]{:T(128)}) %tuple.173), condition=%wide.while_cond, body=%wide.while_body.sunk | while | flops 2 | bytes 21609 | solution.py:137
  600.3 4.5 fusion.180
  604.8 5.2 subtract_multiply_fusion.4
  620.5 4.5 fusion.188
  625.1 32.7 %while.31 = (s32[]{:T(128)}, f32[4352]{0:T(1024)}, s32[16,1]{0,1:T(1,128)S(1)}, f32[16,384]{1,0:T(8,128)S(1)}, s32[]{:T(128)}, /*index=5*/s32[]{:T(128)}) while((s32[]{:T(128)}, f32[4352]{0:T(1024)}, s32[16,1]{0,1:T(1,128)S(1)}, f32[16,384]{1,0:T(8,128)S(1)}, s32[]{:T(128)}, /*index=5*/s32[]{:T(128)}) %tuple.176), condition=%wide.while_cond.1, body=%wide.while_body.1.sunk | while | flops 2 | bytes 9313 | solution.py:138
  658.5 32.7 %while.30 = (s32[]{:T(128)}, f32[6,4352]{1,0:T(8,128)}, s32[16,2]{0,1:T(2,128)S(1)}, f32[16,6,384]{2,1,0:T(8,128)S(1)}, s32[]{:T(128)}) while((s32[]{:T(128)}, f32[6,4352]{1,0:T(8,128)}, s32[16,2]{0,1:T(2,128)S(1)}, f32[16,6,384]{2,1,0:T(8,128)S(1)}, s32[]{:T(128)}) %tuple.173), condition=%wide.while_cond, body=%wide.while_body.sunk | while | flops 2 | bytes 21609 | solution.py:137
  693.4 4.5 fusion.180
  698.0 5.2 subtract_multiply_fusion.4
  713.7 4.5 fusion.188
  (478 shorter events, 274.9 us)
Async XLA Ops:
  2.3 0.5 copy-start.10
  3.7 53.0 %all-to-all-start = ((s32[32,1,12]{2,1,0:T(1,128)}), s32[32,1,12]{2,1,0:T(1,128)S(1)}, u32[]{:S(2)}, u32[]{:S(2)}) async-start(s32[32,1,12]{2,1,0:T(1,128)} %bitcast.65), calls=%async_computation | async-start | bytes 32768 | tf_op jit(solution)/shard_map/all_to_all | solution.py:84
  55.7 10.3 %copy-start.4 = (f32[3,4096]{1,0:T(4,128)}, f32[3,4096]{1,0:T(4,128)S(1)}, u32[]{:S(2)}) copy-start(f32[3,4096]{1,0:T(4,128)S(1)} %broadcast_multiply_fusion.3) | copy-start | bytes 147460
  56.6 19.8 %copy-start.2 = (f32[32,6,128]{2,1,0:T(8,128)}, f32[32,6,128]{2,1,0:T(8,128)S(1)}, u32[]{:S(2)}) copy-start(f32[32,6,128]{2,1,0:T(8,128)S(1)} %fusion.88) | copy-start | bytes 294916
  58.0 8.1 %copy-start.6 = (f32[3,4096]{1,0:T(4,128)S(1)}, f32[3,4096]{1,0:T(4,128)}, u32[]{:S(2)}) copy-start(f32[3,4096]{1,0:T(4,128)} %param.12) | copy-start | bytes 147460
  58.0 16.0 %copy-start.15 = (s32[256]{0:T(256)S(1)}, s32[256]{0:T(256)}, u32[]{:S(2)}) copy-start(s32[256]{0:T(256)} %param.18) | copy-start | bytes 3076
  58.0 16.0 %copy-start.9 = (s32[256,1]{0,1:T(1,128)S(1)}, s32[256,1]{0,1:T(1,128)}, u32[]{:S(2)}) copy-start(s32[256,1]{0,1:T(1,128)} %param.16) | copy-start | bytes 3076
  61.6 43.3 %all-to-all-start.1 = ((f32[32,12,6,128]{3,2,1,0:T(8,128)}), f32[32,12,6,128]{3,2,1,0:T(8,128)S(1)}, u32[]{:S(2)}, u32[]{:S(2)}) async-start(f32[32,12,6,128]{3,2,1,0:T(8,128)} %broadcast_multiply_fusion.1), calls=%async_computation.1 | async-start | bytes 3145728 | tf_op jit(solution)/shard_map/all_to_all | solution.py:88
  66.7 11.6 %collective-permute-start = (f32[6,128]{1,0:T(8,128)}, f32[6,128]{1,0:T(8,128)}, u32[]{:S(2)}, u32[]{:S(2)}) collective-permute-start(f32[6,128]{1,0:T(8,128)} %get-tuple-element.226), channel_id=1, source_target_pairs={{0,1},{1,2},{2,3},{3,4},{4,5},{5,6},{6,7},{8,9},{9,10},{10,11},{11... | collective-permute-start | bytes 9224 | tf_op jit(solution)/shard_map/ppermute | solution.py:21
  70.9 7.3 %collective-permute-start.1 = (f32[6,128]{1,0:T(8,128)}, f32[6,128]{1,0:T(8,128)}, u32[]{:S(2)}, u32[]{:S(2)}) collective-permute-start(f32[6,128]{1,0:T(8,128)} %get-tuple-element.227), channel_id=1, source_target_pairs={{1,0},{2,1},{3,2},{4,3},{5,4},{6,5},{7,6},{9,8},{10,9},{11,10},{12... | collective-permute-start | bytes 9224 | tf_op jit(solution)/shard_map/ppermute | solution.py:23
  107.1 416.9 %copy-start.13 = (f32[4,64]{1,0:T(4,128)S(1)}, f32[4,64]{1,0:T(4,128)}, u32[]{:S(2)}) copy-start(f32[4,64]{1,0:T(4,128)} %fusion.97) | copy-start | bytes 3076
  107.1 418.2 %copy-start.8 = (s32[32,12]{0,1:T(8,128)S(1)}, s32[32,12]{0,1:T(8,128)}, u32[]{:S(2)}) copy-start(s32[32,12]{0,1:T(8,128)} %multiply_add_fusion) | copy-start | bytes 4612
  107.1 418.2 %copy-start.11 = (s32[256]{0:T(256)S(1)}, s32[256]{0:T(256)}, u32[]{:S(2)}) copy-start(s32[256]{0:T(256)} %copy-done.10) | copy-start | bytes 3076
  112.7 26.1 %copy-start.1 = (f32[64,128,128]{2,1,0:T(8,128)}, f32[64,128,128]{2,1,0:T(8,128)S(1)}, u32[]{:S(2)}) copy-start(f32[64,128,128]{2,1,0:T(8,128)S(1)} %multiply_reduce_fusion.13) | copy-start | bytes 12582916 | tf_op jit(solution)/shard_map/while
  147.6 9.2 %copy-start = (f32[64,128,128]{1,2,0:T(8,128)S(1)}, f32[64,128,128]{1,2,0:T(8,128)}, u32[]{:S(2)}) copy-start(f32[64,128,128]{1,2,0:T(8,128)} %copy.502) | copy-start | bytes 12582916 | tf_op jit(solution)/shard_map/while
  212.5 26.1 %copy-start.1 = (f32[64,128,128]{2,1,0:T(8,128)}, f32[64,128,128]{2,1,0:T(8,128)S(1)}, u32[]{:S(2)}) copy-start(f32[64,128,128]{2,1,0:T(8,128)S(1)} %multiply_reduce_fusion.13) | copy-start | bytes 12582916 | tf_op jit(solution)/shard_map/while
  247.5 9.2 %copy-start = (f32[64,128,128]{1,2,0:T(8,128)S(1)}, f32[64,128,128]{1,2,0:T(8,128)}, u32[]{:S(2)}) copy-start(f32[64,128,128]{1,2,0:T(8,128)} %copy.502) | copy-start | bytes 12582916 | tf_op jit(solution)/shard_map/while
  312.4 26.1 %copy-start.1 = (f32[64,128,128]{2,1,0:T(8,128)}, f32[64,128,128]{2,1,0:T(8,128)S(1)}, u32[]{:S(2)}) copy-start(f32[64,128,128]{2,1,0:T(8,128)S(1)} %multiply_reduce_fusion.13) | copy-start | bytes 12582916 | tf_op jit(solution)/shard_map/while
  347.3 9.2 %copy-start = (f32[64,128,128]{1,2,0:T(8,128)S(1)}, f32[64,128,128]{1,2,0:T(8,128)}, u32[]{:S(2)}) copy-start(f32[64,128,128]{1,2,0:T(8,128)} %copy.502) | copy-start | bytes 12582916 | tf_op jit(solution)/shard_map/while
  412.2 26.1 %copy-start.1 = (f32[64,128,128]{2,1,0:T(8,128)}, f32[64,128,128]{2,1,0:T(8,128)S(1)}, u32[]{:S(2)}) copy-start(f32[64,128,128]{2,1,0:T(8,128)S(1)} %multiply_reduce_fusion.13) | copy-start | bytes 12582916 | tf_op jit(solution)/shard_map/while
  447.2 9.2 %copy-start = (f32[64,128,128]{1,2,0:T(8,128)S(1)}, f32[64,128,128]{1,2,0:T(8,128)}, u32[]{:S(2)}) copy-start(f32[64,128,128]{1,2,0:T(8,128)} %copy.502) | copy-start | bytes 12582916 | tf_op jit(solution)/shard_map/while
  525.3 6.5 copy-start.3
  525.3 6.5 copy-start.7
  525.3 6.5 copy-start.14
  528.4 190.5 %all-to-all-start.2 = ((f32[32,12,6,128]{3,2,1,0:T(8,128)}), f32[32,12,6,128]{3,2,1,0:T(8,128)S(1)}, u32[]{:S(2)}, u32[]{:S(2)}) async-start(f32[32,12,6,128]{3,2,1,0:T(8,128)} %copy.348), calls=%async_computation.2 | async-start | bytes 3145728 | tf_op jit(solution)/shard_map/all_to_all | solution.py:92
  531.8 186.4 %copy-start.5 = (f32[4,64,6,128]{3,1,0,2:T(8,128)S(1)}, f32[4,64,6,128]{3,1,0,2:T(8,128)}, u32[]{:S(2)}) copy-start(f32[4,64,6,128]{3,1,0,2:T(8,128)} %get-tuple-element.63) | copy-start | bytes 2359300
  531.8 186.4 %copy-start.17 = (f32[256]{0:T(256)S(1)}, f32[256]{0:T(256)}, u32[]{:S(2)}) copy-start(f32[256]{0:T(256)} %compare_convert_fusion.1) | copy-start | bytes 3076
  531.9 186.5 %copy-start.16 = (s32[256]{0:T(256)S(1)}, s32[256]{0:T(256)}, u32[]{:S(2)}) copy-start(s32[256]{0:T(256)} %param.18) | copy-start | bytes 3076
  531.9 187.0 %copy-start.12 = (s32[384]{0:T(512)S(1)}, s32[384]{0:T(512)}, u32[]{:S(2)}) copy-start(s32[384]{0:T(512)} %eq.96) | copy-start | bytes 4612
where the time goes:
time: 731 us; the launch traced here: 721 us
  matrix products  352 us (48%)
  local copies, waits for them, and re-layouts  193 us (26%)
  other arithmetic  67.8 us (9%)
  blocking collectives  40.5 us (6%)
  waiting for transfers between devices  25.1 us (3%)
  starting transfers between devices  20.7 us (3%)
  loops' own time  19.9 us (3%)
    dot_general x50, matrix products, contract(): return jnp.einsum('ts,cs->ct', matrix, values, precision=highest)  264 us
    gather x224, local copies, waits for them, and re-layouts  130 us
    dot_general x10, matrix products, toward(): jnp.einsum('ct,cs->ts', target_str, source_pos, precision=highest)  85.9 us
    psum x1, blocking collectives, local(): lax.psum((jnp.sum(member * magnitude[:, None], axis=0), jnp.sum(member, a...  40.5 us
    all_to_all x1, waiting for transfers between devices, send_blocks(): lax.all_to_all(outgoing, ('rotor', 'blk'), split_axis=0, concat_axis=0, t...  25.1 us
    mul x4, local copies, waits for them, and re-layouts, kernels(): 3.0 * green_kernel * inverse  22.5 us
    div x4, local copies, waits for them, and re-layouts, kernels(): inverse = 1.0 / (distance_sq + core_square)  22.4 us
    reduce_sum x6, other arithmetic, kernels(): distance_sq = jnp.sum(offset_vec * offset_vec, axis=0)  19.6 us
  transfers between devices with their start and end apart: 5, of which 1 were waited for; matrix products, arithmetic and copies ran while one was open for 28% of the time, Pallas kernels for 0%

commit v1 on v0

--- a/solution.py
+++ b/solution.py
@@ -114,8 +114,10 @@
         blade_of_block[:, None] == jnp.arange(circulation.shape[0], dtype=jnp.int32)[None, :]
     ).astype(jnp.float32)
     totals, counted = lax.psum(
-        (jnp.sum(member * magnitude[:, None], axis=0), jnp.sum(member, axis=0) * width),
-        ("rotor", "blk"),
+        lax.psum(
+            (jnp.sum(member * magnitude[:, None], axis=0), jnp.sum(member, axis=0) * width), "blk"
+        ),
+        "rotor",
     )
     factor = circulation / (totals / jnp.maximum(counted, 1.0) + 1e-06)
     block_factor = jnp.sum(member * factor[None, :], axis=1)

time: 731 us -> 771 us (1.055)
  local copies, waits for them, and re-layouts: 193 us -> 234 us
  blocking collectives: 40.5 us -> 27.3 us
  other arithmetic: 67.8 us -> 75.7 us
    gather x224, local copies, waits for them, and re-layouts: 130 us -> 168 us
    psum x1, blocking collectives: 40.5 us -> 21.7 us  [local(): lax.psum((jnp.sum(member * magnitude[:, None], axis=0), jnp.sum(member, a...]
  transfers between devices with their start and end apart: 5 -> 5, of which waited for: 1 -> 1; matrix products, arithmetic and copies ran while one was open for 28% -> 33% of each run, Pallas kernels for 0% -> 0%
where the time goes in v1:
time: 771 us; the launch traced here: 759 us
  matrix products  356 us (46%)
  local copies, waits for them, and re-layouts  234 us (30%)
  other arithmetic  75.7 us (10%)
  blocking collectives  27.3 us (4%)
  waiting for transfers between devices  25.1 us (3%)
  loops' own time  20.4 us (3%)
  starting transfers between devices  18.8 us (2%)
    dot_general x50, matrix products, contract(): return jnp.einsum('ts,cs->ct', matrix, values, precision=highest)  267 us
    gather x224, local copies, waits for them, and re-layouts  168 us
    dot_general x10, matrix products, toward(): jnp.einsum('ct,cs->ts', target_str, source_pos, precision=highest)  84.9 us
    all_to_all x1, waiting for transfers between devices, send_blocks(): lax.all_to_all(outgoing, ('rotor', 'blk'), split_axis=0, concat_axis=0, t...  25.1 us
    div x4, local copies, waits for them, and re-layouts, kernels(): inverse = 1.0 / (distance_sq + core_square)  22.4 us
    mul x4, local copies, waits for them, and re-layouts, kernels(): 3.0 * green_kernel * inverse  22.4 us
    psum x1, blocking collectives, local(): lax.psum((jnp.sum(member * magnitude[:, None], axis=0), jnp.sum(member, a...  21.7 us
    reduce_sum x6, other arithmetic, kernels(): distance_sq = jnp.sum(offset_vec * offset_vec, axis=0)  21.1 us
  transfers between devices with their start and end apart: 5, of which 1 were waited for; matrix products, arithmetic and copies ran while one was open for 33% of the time, Pallas kernels for 0%

profile of v1, /device:TPU:0, one launch (start us, length us, event | category | flops | bytes accessed | tf_op | source)
XLA Modules:
  0.0 759.4 jit_solution(12117721917894473302)
XLA Ops:
  3.7 7.3 all-to-all-start
  12.7 21.7 %all-reduce.2 = (f32[30]{0:T(128)S(1)}, f32[30]{0:T(128)S(1)}) all-reduce(f32[30]{0:T(128)S(1)} %get-tuple-element.104, f32[30]{0:T(128)S(1)} %broadcast_multiply_fusion.4), channel_id=1, replica_groups=mesh['rotor'=4,'blk'=8] {'blk'}, use_global_device_ids=true, to_apply=%region_3.0 | all-reduce | flops 60 | bytes 480 | tf_op jit(solution)/shard_map/psum | solution.py:117
  34.4 5.6 all-reduce.3
  64.8 25.1 %all-to-all-done.1 = f32[32,12,6,128]{3,2,1,0:T(8,128)S(1)} async-done(((f32[32,12,6,128]{3,2,1,0:T(8,128)}), f32[32,12,6,128]{3,2,1,0:T(8,128)S(1)}, u32[]{:S(2)}, u32[]{:S(2)}) %all-to-all-start.1) | async-done | bytes 1179680 | tf_op jit(solution)/shard_map/all_to_all | solution.py:88
  92.1 417.6 %while.29 = (s32[]{:T(128)}, f32[4,64,6,128]{3,1,0,2:T(8,128)}, f32[4,64,6,128]{3,1,0,2:T(8,128)}, f32[4,64,6,128]{3,1,2,0:T(8,128)}, f32[4,64,6,128]{3,1,2,0:T(8,128)S(1)}, /*index=5*/s32[]{:T(128)}) while((s32[]{:T(128)}, f32[4,64,6,128]{3,1,0,2:T(8,128)}, f32[4,64,6,128]{3,1,0,2:T(8,128)}, f32[4,64,6,128]{3,1,2,0:T(8,128)}, ...), condition=%wide.region_22.23_spmd, body=%wide.region_16.22_spmd.sunk | while | flops 495419392 | bytes 178160320 | solution.py:176
  101.1 5.6 copy.502
  106.7 9.4 %fusion.212 = f32[64,3,128]{2,1,0:T(4,128)S(1)} fusion(f32[64,128,128]{1,2,0:T(8,128)} %copy.502, f32[64,3,128]{2,0,1:T(8,128)S(1)} %get-tuple-element.474), kind=kOutput, calls=%fused_computation.20.clone.1 | convolution fusion | flops 39845888 | bytes 4390912 | tf_op jit(solution)/shard_map/while/body/eval_jaxpr/vmap(ts,cs->ct)/dot_general | solution.py:41
  116.3 7.2 fusion.224
  123.5 8.4 %fusion.214 = f32[64,128,128]{1,2,0:T(8,128)S(1)} fusion(f32[64,128]{1,0:T(8,128)S(1)} %get-tuple-element.492, f32[64,3,128]{2,0,1:T(8,128)S(1)} %get-tuple-element.475, f32[64,3,128]{2,0,1:T(8,128)S(1)} %get-tuple-element.471, f32[64,128,128]{2,1,0:T(8,128)S(1)} %copy-done.2), kind=kOutput, calls=%fused_computation.10.clone.1 | convolution fusion | flops 46137344 | bytes 8617984 | tf_op jit(solution)/shard_map/while/body/eval_jaxpr/vmap(ct,cs->ts)/dot_general | solution.py:58
  143.1 4.5 fusion.219
  147.6 4.5 fusion.209
  155.5 5.6 copy.503
  161.1 10.2 %subtract_multiply_fusion.5 = f32[64,128,128]{2,1,0:T(8,128)S(1)} fusion(f32[64,128,128]{2,1,0:T(8,128)} %copy.503, f32[64,128]{1,0:T(8,128)S(1)} %get-tuple-element.473, f32[64,3,128]{2,0,1:T(8,128)S(1)} %get-tuple-element.474, f32[64,3,128]{2,0,1:T(8,128)S(1)} %get-tuple-element.470, f32[64,128,128]{2,1,0:T(8,128)} %copy-done.1), kind=kOutput, calls=%fused_computation.12.clone.1 | convolution fusion | flops 42991616 | bytes 12812288 | tf_op jit(solution)/shard_map/while/body/eval_jaxpr/vmap(ct,cs->ts)/dot_general | solution.py:58
  171.4 6.6 fusion.217
  178.0 6.6 fusion.207
  184.7 6.6 fusion.211
  201.1 5.6 copy.502
  206.7 9.4 %fusion.212 = f32[64,3,128]{2,1,0:T(4,128)S(1)} fusion(f32[64,128,128]{1,2,0:T(8,128)} %copy.502, f32[64,3,128]{2,0,1:T(8,128)S(1)} %get-tuple-element.474), kind=kOutput, calls=%fused_computation.20.clone.1 | convolution fusion | flops 39845888 | bytes 4390912 | tf_op jit(solution)/shard_map/while/body/eval_jaxpr/vmap(ts,cs->ct)/dot_general | solution.py:41
  216.3 7.2 fusion.224
  223.5 8.4 %fusion.214 = f32[64,128,128]{1,2,0:T(8,128)S(1)} fusion(f32[64,128]{1,0:T(8,128)S(1)} %get-tuple-element.492, f32[64,3,128]{2,0,1:T(8,128)S(1)} %get-tuple-element.475, f32[64,3,128]{2,0,1:T(8,128)S(1)} %get-tuple-element.471, f32[64,128,128]{2,1,0:T(8,128)S(1)} %copy-done.2), kind=kOutput, calls=%fused_computation.10.clone.1 | convolution fusion | flops 46137344 | bytes 8617984 | tf_op jit(solution)/shard_map/while/body/eval_jaxpr/vmap(ct,cs->ts)/dot_general | solution.py:58
  243.1 4.5 fusion.219
  247.6 4.5 fusion.209
  255.5 5.6 copy.503
  261.1 10.2 %subtract_multiply_fusion.5 = f32[64,128,128]{2,1,0:T(8,128)S(1)} fusion(f32[64,128,128]{2,1,0:T(8,128)} %copy.503, f32[64,128]{1,0:T(8,128)S(1)} %get-tuple-element.473, f32[64,3,128]{2,0,1:T(8,128)S(1)} %get-tuple-element.474, f32[64,3,128]{2,0,1:T(8,128)S(1)} %get-tuple-element.470, f32[64,128,128]{2,1,0:T(8,128)} %copy-done.1), kind=kOutput, calls=%fused_computation.12.clone.1 | convolution fusion | flops 42991616 | bytes 12812288 | tf_op jit(solution)/shard_map/while/body/eval_jaxpr/vmap(ct,cs->ts)/dot_general | solution.py:58
  271.4 6.6 fusion.217
  278.0 6.6 fusion.207
  284.7 6.6 fusion.211
  293.8 4.1 multiply_reduce_fusion.13
  301.1 5.6 copy.502
  306.7 9.4 %fusion.212 = f32[64,3,128]{2,1,0:T(4,128)S(1)} fusion(f32[64,128,128]{1,2,0:T(8,128)} %copy.502, f32[64,3,128]{2,0,1:T(8,128)S(1)} %get-tuple-element.474), kind=kOutput, calls=%fused_computation.20.clone.1 | convolution fusion | flops 39845888 | bytes 4390912 | tf_op jit(solution)/shard_map/while/body/eval_jaxpr/vmap(ts,cs->ct)/dot_general | solution.py:41
  316.3 7.2 fusion.224
  323.5 8.4 %fusion.214 = f32[64,128,128]{1,2,0:T(8,128)S(1)} fusion(f32[64,128]{1,0:T(8,128)S(1)} %get-tuple-element.492, f32[64,3,128]{2,0,1:T(8,128)S(1)} %get-tuple-element.475, f32[64,3,128]{2,0,1:T(8,128)S(1)} %get-tuple-element.471, f32[64,128,128]{2,1,0:T(8,128)S(1)} %copy-done.2), kind=kOutput, calls=%fused_computation.10.clone.1 | convolution fusion | flops 46137344 | bytes 8617984 | tf_op jit(solution)/shard_map/while/body/eval_jaxpr/vmap(ct,cs->ts)/dot_general | solution.py:58
  343.1 4.5 fusion.219
  347.6 4.5 fusion.209
  355.5 5.6 copy.503
  361.1 10.2 %subtract_multiply_fusion.5 = f32[64,128,128]{2,1,0:T(8,128)S(1)} fusion(f32[64,128,128]{2,1,0:T(8,128)} %copy.503, f32[64,128]{1,0:T(8,128)S(1)} %get-tuple-element.473, f32[64,3,128]{2,0,1:T(8,128)S(1)} %get-tuple-element.474, f32[64,3,128]{2,0,1:T(8,128)S(1)} %get-tuple-element.470, f32[64,128,128]{2,1,0:T(8,128)} %copy-done.1), kind=kOutput, calls=%fused_computation.12.clone.1 | convolution fusion | flops 42991616 | bytes 12812288 | tf_op jit(solution)/shard_map/while/body/eval_jaxpr/vmap(ct,cs->ts)/dot_general | solution.py:58
  371.4 6.6 fusion.217
  378.0 6.6 fusion.207
  384.7 6.6 fusion.211
  393.8 4.1 multiply_reduce_fusion.13
  401.1 5.6 copy.502
  406.7 9.4 %fusion.212 = f32[64,3,128]{2,1,0:T(4,128)S(1)} fusion(f32[64,128,128]{1,2,0:T(8,128)} %copy.502, f32[64,3,128]{2,0,1:T(8,128)S(1)} %get-tuple-element.474), kind=kOutput, calls=%fused_computation.20.clone.1 | convolution fusion | flops 39845888 | bytes 4390912 | tf_op jit(solution)/shard_map/while/body/eval_jaxpr/vmap(ts,cs->ct)/dot_general | solution.py:41
  416.3 7.2 fusion.224
  423.5 8.4 %fusion.214 = f32[64,128,128]{1,2,0:T(8,128)S(1)} fusion(f32[64,128]{1,0:T(8,128)S(1)} %get-tuple-element.492, f32[64,3,128]{2,0,1:T(8,128)S(1)} %get-tuple-element.475, f32[64,3,128]{2,0,1:T(8,128)S(1)} %get-tuple-element.471, f32[64,128,128]{2,1,0:T(8,128)S(1)} %copy-done.2), kind=kOutput, calls=%fused_computation.10.clone.1 | convolution fusion | flops 46137344 | bytes 8617984 | tf_op jit(solution)/shard_map/while/body/eval_jaxpr/vmap(ct,cs->ts)/dot_general | solution.py:58
  443.1 4.5 fusion.219
  447.6 4.5 fusion.209
  455.5 5.6 copy.503
  461.2 10.2 %subtract_multiply_fusion.5 = f32[64,128,128]{2,1,0:T(8,128)S(1)} fusion(f32[64,128,128]{2,1,0:T(8,128)} %copy.503, f32[64,128]{1,0:T(8,128)S(1)} %get-tuple-element.473, f32[64,3,128]{2,0,1:T(8,128)S(1)} %get-tuple-element.474, f32[64,3,128]{2,0,1:T(8,128)S(1)} %get-tuple-element.470, f32[64,128,128]{2,1,0:T(8,128)} %copy-done.1), kind=kOutput, calls=%fused_computation.12.clone.1 | convolution fusion | flops 42991616 | bytes 12812288 | tf_op jit(solution)/shard_map/while/body/eval_jaxpr/vmap(ct,cs->ts)/dot_general | solution.py:58
  471.4 6.6 fusion.217
  478.0 6.6 fusion.207
  484.7 6.6 fusion.211
  517.6 235.7 %while.28 = (s32[]{:T(128)}, f32[2,16,6,128]{3,1,0,2:T(8,128)}, s32[2,16]{1,0:T(2,128)}, f32[6,4352]{1,0:T(8,128)}, f32[32,6,128]{2,1,0:T(8,128)S(1)}, /*index=5...) while((s32[]{:T(128)}, f32[2,16,6,128]{3,1,0,2:T(8,128)}, ...), condition=%wide.region_13.14_spmd, body=%wide.region_9.13_spmd.sunk | while | flops 192960656 | bytes 30653940 | solution.py:144
  518.3 32.5 %while.30 = (s32[]{:T(128)}, f32[6,4352]{1,0:T(8,128)}, s32[16,2]{0,1:T(2,128)S(1)}, f32[16,6,384]{2,1,0:T(8,128)S(1)}, s32[]{:T(128)}) while((s32[]{:T(128)}, f32[6,4352]{1,0:T(8,128)}, s32[16,2]{0,1:T(2,128)S(1)}, f32[16,6,384]{2,1,0:T(8,128)S(1)}, s32[]{:T(128)}) %tuple.173), condition=%wide.while_cond, body=%wide.while_body.sunk | while | flops 2 | bytes 21601 | solution.py:139
  554.3 5.1 subtract_multiply_fusion.4
  562.9 4.5 fusion.180
  568.3 5.1 fusion.188
  577.5 51.8 %while.31 = (s32[]{:T(128)}, f32[4352]{0:T(1024)}, s32[16,1]{0,1:T(1,128)S(1)}, f32[16,384]{1,0:T(8,128)}, s32[]{:T(128)}, /*index=5*/s32[]{:T(128)}) while((s32[]{:T(128)}, f32[4352]{0:T(1024)}, s32[16,1]{0,1:T(1,128)S(1)}, f32[16,384]{1,0:T(8,128)}, s32[]{:T(128)}, /*index=5*/s32[]{:T(128)}) %tuple.176), condition=%wide.while_cond.1, body=%wide.while_body.1.sunk | while | flops 2 | bytes 9305 | solution.py:140
  630.5 4.3 fusion.187
  636.1 32.5 %while.30 = (s32[]{:T(128)}, f32[6,4352]{1,0:T(8,128)}, s32[16,2]{0,1:T(2,128)S(1)}, f32[16,6,384]{2,1,0:T(8,128)S(1)}, s32[]{:T(128)}) while((s32[]{:T(128)}, f32[6,4352]{1,0:T(8,128)}, s32[16,2]{0,1:T(2,128)S(1)}, f32[16,6,384]{2,1,0:T(8,128)S(1)}, s32[]{:T(128)}) %tuple.173), condition=%wide.while_cond, body=%wide.while_body.sunk | while | flops 2 | bytes 21601 | solution.py:139
  672.2 5.1 subtract_multiply_fusion.4
  680.8 4.5 fusion.180
  686.1 5.1 fusion.188
  695.3 51.8 %while.31 = (s32[]{:T(128)}, f32[4352]{0:T(1024)}, s32[16,1]{0,1:T(1,128)S(1)}, f32[16,384]{1,0:T(8,128)}, s32[]{:T(128)}, /*index=5*/s32[]{:T(128)}) while((s32[]{:T(128)}, f32[4352]{0:T(1024)}, s32[16,1]{0,1:T(1,128)S(1)}, f32[16,384]{1,0:T(8,128)}, s32[]{:T(128)}, /*index=5*/s32[]{:T(128)}) %tuple.176), condition=%wide.while_cond.1, body=%wide.while_body.1.sunk | while | flops 2 | bytes 9305 | solution.py:140
  748.4 4.3 fusion.187
  (487 shorter events, 330.3 us)
Async XLA Ops:
  2.3 0.5 copy-start.11
  3.7 39.7 %all-to-all-start = ((s32[32,1,12]{2,1,0:T(1,128)}), s32[32,1,12]{2,1,0:T(1,128)S(1)}, u32[]{:S(2)}, u32[]{:S(2)}) async-start(s32[32,1,12]{2,1,0:T(1,128)} %bitcast.65), calls=%async_computation | async-start | bytes 32768 | tf_op jit(solution)/shard_map/all_to_all | solution.py:84
  42.5 8.6 %copy-start.6 = (f32[3,4096]{1,0:T(4,128)}, f32[3,4096]{1,0:T(4,128)S(1)}, u32[]{:S(2)}) copy-start(f32[3,4096]{1,0:T(4,128)S(1)} %broadcast_multiply_fusion.3) | copy-start | bytes 147460
  43.4 17.9 %copy-start.4 = (f32[32,6,128]{2,1,0:T(8,128)}, f32[32,6,128]{2,1,0:T(8,128)S(1)}, u32[]{:S(2)}) copy-start(f32[32,6,128]{2,1,0:T(8,128)S(1)} %fusion.88) | copy-start | bytes 294916
  44.8 6.3 copy-start.8
  44.8 14.1 %copy-start.10 = (s32[256,1]{0,1:T(1,128)S(1)}, s32[256,1]{0,1:T(1,128)}, u32[]{:S(2)}) copy-start(s32[256,1]{0,1:T(1,128)} %param.16) | copy-start | bytes 3076
  44.8 14.7 %copy-start.14 = (s32[256]{0:T(256)S(1)}, s32[256]{0:T(256)}, u32[]{:S(2)}) copy-start(s32[256]{0:T(256)} %param.18) | copy-start | bytes 3076
  48.3 41.5 %all-to-all-start.1 = ((f32[32,12,6,128]{3,2,1,0:T(8,128)}), f32[32,12,6,128]{3,2,1,0:T(8,128)S(1)}, u32[]{:S(2)}, u32[]{:S(2)}) async-start(f32[32,12,6,128]{3,2,1,0:T(8,128)} %broadcast_multiply_fusion.1), calls=%async_computation.1 | async-start | bytes 3145728 | tf_op jit(solution)/shard_map/all_to_all | solution.py:88
  51.7 11.5 %collective-permute-start = (f32[6,128]{1,0:T(8,128)}, f32[6,128]{1,0:T(8,128)}, u32[]{:S(2)}, u32[]{:S(2)}) collective-permute-start(f32[6,128]{1,0:T(8,128)} %get-tuple-element.228), channel_id=1, source_target_pairs={{0,1},{1,2},{2,3},{3,4},{4,5},{5,6},{6,7},{8,9},{9,10},{10,11},{11... | collective-permute-start | bytes 9224 | tf_op jit(solution)/shard_map/ppermute | solution.py:21
  55.8 7.4 collective-permute-start.1
  92.1 417.6 %copy-start.13 = (f32[4,64]{1,0:T(4,128)S(1)}, f32[4,64]{1,0:T(4,128)}, u32[]{:S(2)}) copy-start(f32[4,64]{1,0:T(4,128)} %fusion.97) | copy-start | bytes 3076
  92.1 418.9 %copy-start.9 = (s32[32,12]{0,1:T(8,128)S(1)}, s32[32,12]{0,1:T(8,128)}, u32[]{:S(2)}) copy-start(s32[32,12]{0,1:T(8,128)} %multiply_add_fusion) | copy-start | bytes 4612
  92.1 419.0 %copy-start.12 = (s32[256]{0:T(256)S(1)}, s32[256]{0:T(256)}, u32[]{:S(2)}) copy-start(s32[256]{0:T(256)} %copy-done.11) | copy-start | bytes 3076
  97.9 3.2 copy-start.1
  106.7 9.6 %copy-start = (f32[64,128,128]{1,2,0:T(8,128)S(1)}, f32[64,128,128]{1,2,0:T(8,128)}, u32[]{:S(2)}) copy-start(f32[64,128,128]{1,2,0:T(8,128)} %copy.502) | copy-start | bytes 12582916 | tf_op jit(solution)/shard_map/while
  106.7 16.8 %copy-start.2 = (f32[64,128,128]{2,1,0:T(8,128)S(1)}, f32[64,128,128]{2,1,0:T(8,128)}, u32[]{:S(2)}) copy-start(f32[64,128,128]{2,1,0:T(8,128)} %copy-done.1) | copy-start | bytes 12582916 | tf_op jit(solution)/shard_map/while
  171.4 13.3 %copy-start.3 = (f32[64,128,128]{2,1,0:T(8,128)S(1)}, f32[64,128,128]{2,1,0:T(8,128)}, u32[]{:S(2)}) copy-start(f32[64,128,128]{2,1,0:T(8,128)} %copy-done.1) | copy-start | bytes 12582916 | tf_op jit(solution)/shard_map/while
  197.9 3.2 copy-start.1
  206.7 9.6 %copy-start = (f32[64,128,128]{1,2,0:T(8,128)S(1)}, f32[64,128,128]{1,2,0:T(8,128)}, u32[]{:S(2)}) copy-start(f32[64,128,128]{1,2,0:T(8,128)} %copy.502) | copy-start | bytes 12582916 | tf_op jit(solution)/shard_map/while
  206.7 16.8 %copy-start.2 = (f32[64,128,128]{2,1,0:T(8,128)S(1)}, f32[64,128,128]{2,1,0:T(8,128)}, u32[]{:S(2)}) copy-start(f32[64,128,128]{2,1,0:T(8,128)} %copy-done.1) | copy-start | bytes 12582916 | tf_op jit(solution)/shard_map/while
  271.4 13.3 %copy-start.3 = (f32[64,128,128]{2,1,0:T(8,128)S(1)}, f32[64,128,128]{2,1,0:T(8,128)}, u32[]{:S(2)}) copy-start(f32[64,128,128]{2,1,0:T(8,128)} %copy-done.1) | copy-start | bytes 12582916 | tf_op jit(solution)/shard_map/while
  297.9 3.2 copy-start.1
  306.7 9.6 %copy-start = (f32[64,128,128]{1,2,0:T(8,128)S(1)}, f32[64,128,128]{1,2,0:T(8,128)}, u32[]{:S(2)}) copy-start(f32[64,128,128]{1,2,0:T(8,128)} %copy.502) | copy-start | bytes 12582916 | tf_op jit(solution)/shard_map/while
  306.7 16.8 %copy-start.2 = (f32[64,128,128]{2,1,0:T(8,128)S(1)}, f32[64,128,128]{2,1,0:T(8,128)}, u32[]{:S(2)}) copy-start(f32[64,128,128]{2,1,0:T(8,128)} %copy-done.1) | copy-start | bytes 12582916 | tf_op jit(solution)/shard_map/while
  371.4 13.3 %copy-start.3 = (f32[64,128,128]{2,1,0:T(8,128)S(1)}, f32[64,128,128]{2,1,0:T(8,128)}, u32[]{:S(2)}) copy-start(f32[64,128,128]{2,1,0:T(8,128)} %copy-done.1) | copy-start | bytes 12582916 | tf_op jit(solution)/shard_map/while
  397.9 3.2 copy-start.1
  406.7 9.6 %copy-start = (f32[64,128,128]{1,2,0:T(8,128)S(1)}, f32[64,128,128]{1,2,0:T(8,128)}, u32[]{:S(2)}) copy-start(f32[64,128,128]{1,2,0:T(8,128)} %copy.502) | copy-start | bytes 12582916 | tf_op jit(solution)/shard_map/while
  406.7 16.8 %copy-start.2 = (f32[64,128,128]{2,1,0:T(8,128)S(1)}, f32[64,128,128]{2,1,0:T(8,128)}, u32[]{:S(2)}) copy-start(f32[64,128,128]{2,1,0:T(8,128)} %copy-done.1) | copy-start | bytes 12582916 | tf_op jit(solution)/shard_map/while
  471.4 13.3 %copy-start.3 = (f32[64,128,128]{2,1,0:T(8,128)S(1)}, f32[64,128,128]{2,1,0:T(8,128)}, u32[]{:S(2)}) copy-start(f32[64,128,128]{2,1,0:T(8,128)} %copy-done.1) | copy-start | bytes 12582916 | tf_op jit(solution)/shard_map/while
  511.0 6.5 copy-start.5
  514.1 241.8 %all-to-all-start.2 = ((f32[32,12,6,128]{3,2,1,0:T(8,128)}), f32[32,12,6,128]{3,2,1,0:T(8,128)}, u32[]{:S(2)}, u32[]{:S(2)}) async-start(f32[32,12,6,128]{3,2,1,0:T(8,128)} %copy.348), calls=%async_computation.2 | async-start | bytes 3145728 | tf_op jit(solution)/shard_map/all_to_all | solution.py:92
  629.2 5.5 copy-start.7
  747.1 5.5 copy-start.7
